TPU v7x, 512 devices: a whole 4x4x16 slice. The times are simulated.
512 devices in a mesh: ctx: 16 (over y, x_hi, core), exp: 32 (over z, x_lo).
Axes of the slice: x: 4 (x_hi: 2, x_lo: 2; x = x_hi * 2 + x_lo), y: 4, z: 16, core: 2. Of those that a mesh axis runs over, the one named last changes fastest.
Arguments:
- resid: bfloat16 [32, 256, 4096], P('exp', 'ctx'), may hold values from -4 to 4
- query: bfloat16 [32, 256, 4096], P('exp', 'ctx'), may hold values from -10 to 10
- key_new: bfloat16 [32, 256, 256], P('exp', 'ctx'), may hold values from -6 to 6
- value_new: bfloat16 [32, 256, 256], P('exp', 'ctx'), may hold values from -6 to 6
- cache_key: bfloat16 [32, 2048, 256], P('exp', 'ctx'), may hold values from -240 to 240
- cache_value: bfloat16 [32, 2048, 256], P('exp', 'ctx'), may hold values from -6 to 6
- cache_len: int32 [32], P('exp'), may hold values from 512 to 2048
- block_of: int32 [16], replicated, may hold values from 0 to 15, each once
- out_proj: bfloat16 [4096, 4096], P(None, 'ctx'), may hold values from -0.09375 to 0.09375
- norm_gain: float32 [4096], replicated, may hold values from 0.1 to 1.9
- routes: int32 [32, 256, 8], P('exp', 'ctx'), may hold values from 0 to 127, as said below
- route_logits: float32 [32, 256, 8], P('exp', 'ctx'), may hold values from -12 to 304
- w_gate: bfloat16 [32, 1536, 4096], P('exp', 'ctx'), may hold values from -0.25 to 0.25
- w_up: bfloat16 [32, 1536, 4096], P('exp', 'ctx'), may hold values from -0.25 to 0.25
- w_down: bfloat16 [32, 1536, 4096], P('exp', None, 'ctx'), may hold values from -0.375 to 0.375
Outputs:
- layer_out: bfloat16 [32, 256, 4096], P('exp', 'ctx')
Inputs may be any that keep to these rules, and one draw needn't show every extreme that they name: `routes`: each row names 8 different expert numbers of 0 to 127; only numbers below 32 are experts of this layer slice; among the rows of one device no number appears more than 2 times, and 2 is reached on every device. `block_of`: a permutation.
All inputs are finite; a program needn't handle non-finite values.
Results may differ from a plain program's by a relative error of at most 0.015.
The roundings to bfloat16 on the way count: a program that leaves them out, or rounds other values in their place, can miss the bound.
Values may be sent and summed in bfloat16 or wider, within the bound.
A program may use at most 128 MiB of HBM per device.

v0:
```python
import math

import jax
import jax.numpy as jnp
from jax import lax
from jax.sharding import PartitionSpec as P

HD = 128
CAP = 2


def rotate(vectors, positions):
    half = vectors.shape[-1] // 2
    rates = jnp.exp(
        jnp.arange(half, dtype=jnp.float32) * (-2.0 * math.log(1000000.0) / vectors.shape[-1])
    )
    angles = positions.astype(jnp.float32)[:, None] * rates[None, :]
    cosine = jnp.cos(angles)[:, None, :]
    sine = jnp.sin(angles)[:, None, :]
    first = vectors[..., :half]
    second = vectors[..., half:]
    return jnp.concatenate(
        [first * cosine - second * sine, second * cosine + first * sine], axis=-1
    )


def lookup(table, index):
    match = index[:, None] == jnp.arange(table.shape[0], dtype=jnp.int32)[None, :]
    return jnp.sum(jnp.where(match, table[None, :], 0), axis=1)


def combine(older, newer):
    peak = jnp.maximum(older[0], newer[0])
    later = jnp.exp(newer[0] - peak)
    return (peak, newer[1] * later, newer[2] * later[..., None])


def local(
    resid,
    query,
    key_new,
    value_new,
    cache_key,
    cache_value,
    cache_len,
    block_of,
    out_proj,
    norm_gain,
    routes,
    route_logits,
    w_gate,
    w_up,
    w_down,
):
    count = resid.shape[1]
    stored_rows = cache_key.shape[1]
    kv_heads = cache_key.shape[2] // HD
    query_heads = query.shape[2] // HD
    group = query_heads // kv_heads
    model_width = resid.shape[2]
    shards = lax.axis_size("ctx")
    here = lax.axis_index("ctx")
    length = cache_len[0]
    stride = stored_rows + count
    scale = HD ** (-0.5)
    rows_total = count * group

    def fresh_positions(devices, tokens):
        return length + lookup(block_of, devices) * count + tokens

    positions = fresh_positions(
        jnp.zeros((count,), jnp.int32) + here, jnp.arange(count, dtype=jnp.int32)
    )
    turned = rotate(query[0].astype(jnp.float32).reshape(count, query_heads, HD), positions).astype(
        jnp.bfloat16
    )
    turned = (
        turned.reshape(count, kv_heads, group, HD)
        .transpose(1, 0, 2, 3)
        .reshape(kv_heads, rows_total, HD)
    )
    rotated_keys = rotate(key_new[0].astype(jnp.float32).reshape(count, kv_heads, HD), positions)
    rotated_keys = rotated_keys.astype(jnp.bfloat16).reshape(count, kv_heads * HD)
    own_keys = jnp.concatenate([cache_key[0], rotated_keys], axis=0)
    own_values = jnp.concatenate([cache_value[0], value_new[0]], axis=0)
    row_positions = jnp.repeat(positions, group)
    start_state = (
        jnp.full((kv_heads, rows_total), -1e30, jnp.float32),
        jnp.zeros((kv_heads, rows_total), jnp.float32),
        jnp.zeros((kv_heads, rows_total, HD), jnp.float32),
    )
    keys = lax.all_gather(own_keys, "ctx", axis=0, tiled=True)
    values = lax.all_gather(own_values, "ctx", axis=0, tiled=True)
    index = jnp.arange(keys.shape[0], dtype=jnp.int32)
    device = index // stride
    within = index % stride
    cached = within < stored_rows
    slots = device * stored_rows + within
    key_positions = fresh_positions(device, within - stored_rows)
    keys_split = keys.reshape(keys.shape[0], kv_heads, HD)
    values_split = values.reshape(values.shape[0], kv_heads, HD)
    scores = (
        jnp.einsum("hqd,khd->hqk", turned, keys_split, preferred_element_type=jnp.float32) * scale
    )
    visible = jnp.where(
        cached[None, :], (slots < length)[None, :], key_positions[None, :] <= row_positions[:, None]
    )[None]
    scores = jnp.where(visible, scores, -1e30)
    peak = jnp.max(scores, axis=2)
    weights = jnp.where(visible, jnp.exp(scores - peak[..., None]), 0.0)
    summed = jnp.einsum(
        "hqk,khd->hqd",
        weights.astype(jnp.bfloat16),
        values_split,
        preferred_element_type=jnp.float32,
    )
    peak, total, summed = combine(start_state, (peak, jnp.sum(weights, axis=2), summed))
    mixed = (summed / total[..., None]).astype(jnp.bfloat16)
    mixed = (
        mixed.reshape(kv_heads, count, group, HD)
        .transpose(1, 0, 2, 3)
        .reshape(count, query_heads * HD)
    )
    every_mixed = lax.all_gather(mixed, "ctx", axis=0, tiled=True)
    projected = jnp.dot(every_mixed, out_proj, preferred_element_type=jnp.float32)
    attention = lax.all_to_all(
        projected.astype(jnp.bfloat16), "ctx", split_axis=0, concat_axis=1, tiled=True
    ).astype(projected.dtype)
    rounded = lax.optimization_barrier(
        (resid[0].astype(jnp.float32) + attention).astype(jnp.bfloat16)
    )
    stream = rounded.astype(jnp.float32)
    normed = (
        stream * lax.rsqrt(jnp.mean(stream * stream, axis=1, keepdims=True) + 1e-06) * norm_gain
    ).astype(jnp.bfloat16)
    shares = jax.nn.softmax(route_logits[0], axis=1)
    experts_here = lax.axis_size("exp")
    expert_ids = jnp.arange(experts_here, dtype=jnp.int32)
    hits = routes[0][:, :, None] == expert_ids[None, None, :]
    taken = jnp.any(hits, axis=1)
    weight_of = jnp.sum(jnp.where(hits, shares[:, :, None], 0.0), axis=1)
    ranks = jnp.cumsum(taken.astype(jnp.int32), axis=0) - 1
    placed = (ranks.T[:, None, :] == jnp.arange(CAP, dtype=jnp.int32)[None, :, None]) & taken.T[
        :, None, :
    ]
    outgoing = jnp.einsum(
        "est,td->esd", placed.astype(jnp.bfloat16), normed, preferred_element_type=jnp.float32
    ).astype(jnp.bfloat16)
    arrived = lax.all_to_all(outgoing, "exp", split_axis=0, concat_axis=0, tiled=True)
    arrived_rows = arrived.reshape(experts_here * CAP, model_width)
    gate_matrix = w_gate[0]
    up_matrix = w_up[0]
    down_matrix = w_down[0]
    contract = (((1,), (1,)), ((), ()))
    piece = lax.all_gather(arrived_rows, "ctx", axis=0, tiled=True)
    gate = lax.dot_general(piece, gate_matrix, contract, preferred_element_type=jnp.float32)
    upward = lax.dot_general(piece, up_matrix, contract, preferred_element_type=jnp.float32)
    hidden = (jax.nn.silu(gate) * upward).astype(jnp.bfloat16)
    produced = jnp.dot(
        lax.all_gather(hidden, "ctx", axis=1, tiled=True),
        down_matrix,
        preferred_element_type=jnp.float32,
    )
    results = produced.astype(jnp.bfloat16).reshape(shards, experts_here, CAP, down_matrix.shape[1])
    homeward = lax.all_to_all(
        lax.all_to_all(results, "ctx", split_axis=0, concat_axis=3, tiled=True),
        "exp",
        split_axis=1,
        concat_axis=0,
        tiled=True,
    )
    returned = homeward.reshape(experts_here * CAP, model_width).astype(jnp.float32)
    mixing = (placed.astype(jnp.float32) * weight_of.T[:, None, :]).reshape(
        experts_here * CAP, count
    )
    added = lax.dot_general(
        mixing,
        returned,
        (((0,), (0,)), ((), ())),
        precision=lax.Precision.HIGHEST,
        preferred_element_type=jnp.float32,
    )
    return (stream + added).astype(jnp.bfloat16)[None]


def solution(mesh):
    in_specs = (
        P("exp", "ctx", None),
        P("exp", "ctx", None),
        P("exp", "ctx", None),
        P("exp", "ctx", None),
        P("exp", "ctx", None),
        P("exp", "ctx", None),
        P("exp"),
        P(),
        P(None, "ctx"),
        P(),
        P("exp", "ctx", None),
        P("exp", "ctx", None),
        P("exp", "ctx", None),
        P("exp", "ctx", None),
        P("exp", None, "ctx"),
    )
    out_specs = P("exp", "ctx", None)
    return jax.shard_map(local, mesh=mesh, in_specs=in_specs, out_specs=out_specs, check_vma=False)
```

profile of v0, /device:TPU:2, one launch (start us, length us, event | category | flops | bytes accessed | tf_op | source)
XLA Modules:
  0.0 496.2 jit_solution(328826511187318312)
XLA Ops:
  7.4 0.7 reshape.328
  8.1 0.8 select_reduce_fusion.2
  9.2 1.5 pad_maximum_fusion
  10.7 1.5 pad_maximum_fusion.1
  12.3 0.9 convert_bitcast_fusion.1
  13.8 0.8 select_reduce_fusion
  14.6 0.5 compare_select_fusion
  15.1 59.8 %all-gather.6.cloned.1.call-done = bf16[2304,256]{1,0:T(8,128)(2,1)} async-done(((bf16[144,256]{1,0:T(8,128)(2,1)}), bf16[2304,256]{1,0:T(8,128)(2,1)}) %all-gather.6.cloned.1.call-update) | async-done | bytes 1179664 | tf_op jit(solution)/shard_map/all_gather | solution.py:92
  74.9 2.4 copy.95
  77.3 2.5 fusion.47
  79.8 2.1 copy-done.1
  81.9 1.3 fusion.3
  83.2 54.5 %all-gather.8.cloned.1.call-done = bf16[2304,256]{1,0:T(8,128)(2,1)} async-done(((bf16[144,256]{1,0:T(8,128)(2,1)}), bf16[2304,256]{1,0:T(8,128)(2,1)}) %all-gather.8.cloned.1.call-update) | async-done | bytes 1179664 | tf_op jit(solution)/shard_map/all_gather | solution.py:93
  137.7 2.4 copy.97
  140.0 3.6 fusion.17
  143.7 0.7 copy.123
  145.2 61.2 %all-gather.10.cloned.1.call-done = bf16[256,4096]{1,0:T(8,128)(2,1)} async-done(((bf16[16,4096]{1,0:T(8,128)(2,1)}), bf16[256,4096]{1,0:T(8,128)(2,1)}) %all-gather.10.cloned.1.call-update) | async-done | bytes 2097168 | tf_op jit(solution)/shard_map/all_gather | solution.py:124
  206.3 3.0 convolution_convert_fusion.2
  209.3 4.7 all-to-all-start
  214.1 8.1 %all-to-all-done = bf16[16,16,256]{2,1,0:T(8,128)(2,1)S(1)} async-done(((bf16[16,16,256]{2,1,0:T(8,128)(2,1)}), bf16[16,16,256]{2,1,0:T(8,128)(2,1)S(1)}, u32[]{:S(2)}, u32[]{:S(2)}) %all-to-all-start) | async-done | bytes 131104 | tf_op jit(solution)/shard_map/all_to_all | solution.py:126
  222.8 0.5 copy.107
  223.3 46.3 %all_to_all.45 = bf16[32,2,4096]{2,1,0:T(2,128)(2,1)S(1)} all-to-all(bf16[32,2,4096]{2,1,0:T(2,128)(2,1)S(1)} %copy.107), channel_id=1, replica_groups=mesh['ctx'=16,'exp'=32] {'exp'}, dimensions={0} | all-to-all | bytes 1048576 | tf_op jit(solution)/shard_map/all_to_all | solution.py:149
  269.7 1.0 reshape.323
  271.0 75.8 %all-gather.12.cloned.1.call-done = bf16[1024,4096]{1,0:T(8,128)(2,1)} async-done(((bf16[64,4096]{1,0:T(8,128)(2,1)}), bf16[1024,4096]{1,0:T(8,128)(2,1)}) %all-gather.12.cloned.1.call-update) | async-done | bytes 8388624 | tf_op jit(solution)/shard_map/all_gather | solution.py:155
  346.8 6.4 %fusion.22 = f32[1024,96]{0,1:T(8,128)S(1)} fusion(bf16[1024,4096]{1,0:T(8,128)(2,1)} %all-gather.12.cloned.1.call-done, bf16[1,96,4096]{2,1,0:T(8,128)(2,1)} %param.27), kind=kOutput, calls=%fused_computation.23 | convolution fusion | flops 805306368 | bytes 9568256 | tf_op jit(solution)/shard_map/dot_general | solution.py:156
  353.2 3.4 fusion.10
  356.6 64.1 %all-gather.14.cloned.1.call-done = bf16[1024,1536]{0,1:T(8,128)(2,1)} async-done(((bf16[1024,96]{0,1:T(8,128)(2,1)}), bf16[1024,1536]{0,1:T(8,128)(2,1)}) %all-gather.14.cloned.1.call-update) | async-done | bytes 3145744 | tf_op jit(solution)/shard_map/all_gather | solution.py:160
  420.8 3.1 convolution_convert_fusion.1
  424.2 16.8 %all_to_all.46 = bf16[16,32,2,256]{3,1,2,0:T(8,128)(2,1)S(1)} all-to-all(bf16[16,32,2,256]{3,1,2,0:T(8,128)(2,1)S(1)} %copy.108), channel_id=1, replica_groups=mesh['ctx'=16,'exp'=32] {'ctx'}, dimensions={0} | all-to-all | bytes 1048576 | tf_op jit(solution)/shard_map/all_to_all | solution.py:166
  441.4 45.9 %all_to_all.47 = bf16[1,32,2,4096]{3,2,0,1:T(2,128)(2,1)} all-to-all(bf16[1,32,2,4096]{3,2,0,1:T(2,128)(2,1)S(1)} %reshape.331), channel_id=1, replica_groups=mesh['ctx'=16,'exp'=32] {'exp'}, dimensions={1} | all-to-all | bytes 1048576 | tf_op jit(solution)/shard_map/all_to_all | solution.py:165
  487.4 1.2 reshape.325
  488.6 1.0 fusion.2
  (67 shorter events, 3.3 us)
Async XLA Ops:
  6.5 199.8 %copy-start = (bf16[4096,256]{1,0:T(8,128)(2,1)S(1)}, bf16[4096,256]{1,0:T(8,128)(2,1)}, u32[]{:S(2)}) copy-start(bf16[4096,256]{1,0:T(8,128)(2,1)} %param.23) | copy-start | bytes 6291460
  6.5 68.4 %all-gather.6.cloned.1.call-start = ((), (), s32[]{:S(2)}) async-start(), calls=%async_computation.4 | async-start | bytes 1253376 | tf_op jit(solution)/shard_map/all_gather | solution.py:92
  10.7 127.0 %all-gather.8.cloned.1.call-start = ((), (), s32[]{:S(2)}) async-start(), calls=%async_computation.5 | async-start | bytes 1253376 | tf_op jit(solution)/shard_map/all_gather | solution.py:93
  12.3 194.1 %all-gather.10.cloned.1.call-start = ((), (), s32[]{:S(2)}) async-start(), calls=%async_computation.6 | async-start | bytes 2228224 | tf_op jit(solution)/shard_map/all_gather | solution.py:124
  79.8 2.1 copy-start.1
  140.0 4.4 copy-start.4
  140.0 4.5 copy-start.6
  143.7 78.6 %copy-start.3 = (bf16[1,16,4096]{2,1,0:T(8,128)(2,1)S(1)}, bf16[1,16,4096]{2,1,0:T(8,128)(2,1)}, u32[]{:S(2)}) copy-start(bf16[1,16,4096]{2,1,0:T(8,128)(2,1)} %param.15) | copy-start | bytes 393220
  145.2 77.3 %copy-start.5 = (f32[4096]{0:T(1024)S(1)}, f32[4096]{0:T(1024)}, u32[]{:S(2)}) copy-start(f32[4096]{0:T(1024)} %param.24) | copy-start | bytes 49156
  209.3 12.9 %all-to-all-start = ((bf16[16,16,256]{2,1,0:T(8,128)(2,1)}), bf16[16,16,256]{2,1,0:T(8,128)(2,1)S(1)}, u32[]{:S(2)}, u32[]{:S(2)}) async-start(bf16[16,16,256]{2,1,0:T(8,128)(2,1)} %bitcast.13), calls=%async_computation | async-start | bytes 262144 | tf_op jit(solution)/shard_map/all_to_all | solution.py:126
  214.0 132.8 %all-gather.12.cloned.1.call-start = ((), (), s32[]{:S(2)}) async-start(), calls=%async_computation.7 | async-start | bytes 8912896 | tf_op jit(solution)/shard_map/all_gather | solution.py:155
  270.7 82.5 %copy-start.7 = (bf16[1,96,4096]{2,1,0:T(8,128)(2,1)S(1)}, bf16[1,96,4096]{2,1,0:T(8,128)(2,1)}, u32[]{:S(2)}) copy-start(bf16[1,96,4096]{2,1,0:T(8,128)(2,1)} %param.28) | copy-start | bytes 2359300
  270.7 150.0 %all-gather.14.cloned.1.call-start = ((), (), s32[]{:S(2)}) async-start(), calls=%async_computation.8 | async-start | bytes 3342336 | tf_op jit(solution)/shard_map/all_gather | solution.py:160
  346.8 6.4 %copy-start.2 = (bf16[1024,4096]{1,0:T(8,128)(2,1)S(1)}, bf16[1024,4096]{1,0:T(8,128)(2,1)}, u32[]{:S(2)}) copy-start(bf16[1024,4096]{1,0:T(8,128)(2,1)} %all-gather.12.cloned.1.call-done) | copy-start | bytes 25165828
Sparse Core Ops, SparseCore 0:
  10.8 64.0 all-gather.5
  78.2 59.3 all-gather.7
  144.5 61.7 all-gather.9
  270.8 75.9 all-gather.11
  356.8 63.9 all-gather.13
where the time goes:
time: 497 us; the launch traced here: 496 us
  waiting for transfers between devices  324 us (65%)
  blocking collectives  109 us (22%)
  matrix products  23.3 us (5%)
  between operations  14.2 us (3%)
  local copies, waits for them, and re-layouts  12.5 us (3%)
  other arithmetic  8.39 us (2%)
  starting transfers between devices  5.02 us (1%)
    all_gather x1, waiting for transfers between devices, local(): piece = lax.all_gather(arrived_rows, 'ctx', axis=0, tiled=True)  75.8 us
    all_gather x1, waiting for transfers between devices, local(): lax.all_gather(hidden, 'ctx', axis=1, tiled=True)  64.1 us
    all_gather x1, waiting for transfers between devices, local(): every_mixed = lax.all_gather(mixed, 'ctx', axis=0, tiled=True)  61.2 us
    all_gather x1, waiting for transfers between devices, local(): keys = lax.all_gather(own_keys, 'ctx', axis=0, tiled=True)  59.8 us
    all_gather x1, waiting for transfers between devices, local(): values = lax.all_gather(own_values, 'ctx', axis=0, tiled=True)  54.5 us
    all_to_all x1, blocking collectives, local(): lax.all_to_all(outgoing, 'exp', split_axis=0, concat_axis=0, tiled=True)  46.3 us
    all_to_all x1, blocking collectives, local(): lax.all_to_all(lax.all_to_all(results, 'ctx', split_axis=0, concat_axis=3...  45.9 us
    all_to_all x1, blocking collectives, local(): lax.all_to_all(results, 'ctx', split_axis=0, concat_axis=3, tiled=True)  16.8 us
  transfers between devices with their start and end apart: 6, of which 6 were waited for; matrix products, arithmetic and copies ran while one was open for 2% of the time, Pallas kernels for 0%

commit v1 on v0

v1 whole, which is shorter than its diff:
```python
import math

import jax
import jax.numpy as jnp
import numpy as np
from jax import lax
from jax.experimental import pallas as pl
from jax.experimental.pallas import tpu as pltpu
from jax.sharding import PartitionSpec as P

MESH = pl.DeviceIdType.MESH
BF = jnp.bfloat16
F32 = jnp.float32
HD = 128
TOK = 16
CACHED = 128
KEYS = TOK + CACHED
GROUP = 16
PLANES = 8
WIDE = 512
NEXP = 32
UNITS = 96
OFFSETS = ((0, 1, -1, 2), (8, 7, -7, -6), (6, 5, -5, -4), (4, 3, -3, -2))
CHUNKS = len(OFFSETS)
PER = 8
ROWS = PER * 2 * PLANES
YS = (2, 6, 4)
NEG = -1e30
SENDS = 288
RECVS = 320


def iota(shape, axis):
    return lax.broadcasted_iota(jnp.int32, shape, axis)


def onehot(condition):
    return jnp.where(condition, 1.0, 0.0).astype(BF)


def dot(a, b):
    return jnp.dot(a, b, preferred_element_type=F32)


def dot_t(a, b):
    return lax.dot_general(a, b, (((1,), (1,)), ((), ())), preferred_element_type=F32)


def thirds(x):
    high = x.astype(BF)
    rest = x - high.astype(F32)
    middle = rest.astype(BF)
    return high, middle, (rest - middle.astype(F32)).astype(BF)


def kernel(
    length_ref,
    block_ref,
    rates_ref,
    resid_ref,
    query_ref,
    key_new_ref,
    value_new_ref,
    cache_key_ref,
    cache_value_ref,
    gain_ref,
    routes_ref,
    logits_ref,
    out_proj_hbm,
    gate_hbm,
    up_hbm,
    down_hbm,
    out_ref,
    q_buf,
    q_stage,
    kv,
    kv_stage,
    score_buf,
    peak_buf,
    mix,
    w_out,
    part_send,
    part_recv,
    proj_send,
    attn,
    stream_buf,
    info,
    z_send,
    z_recv,
    rows_buf,
    w_gate,
    w_up,
    w_down,
    hid,
    ret_send,
    ret,
    fin_send,
    fin,
    send_sems,
    recv_sems,
    local_sems,
):
    ctx = lax.axis_index("ctx")
    ex = lax.axis_index("exp")
    core, p = lax.rem(ctx, 2), lax.div(ctx, 2)
    y, h = lax.div(p, 2), lax.rem(p, 2)
    z, low = lax.div(ex, 2), lax.rem(ex, 2)
    other = 1 - core
    ys = {0: y, 2: y + 1 - 2 * lax.rem(y, 2), 4: lax.rem(y + 2, 4), 6: 3 - y}
    peer = [2 * ys[i & 6] + ((1 - h) if i & 1 else h) for i in range(PLANES)]
    partner = {"ctx": 2 * p + other}

    def plane(i):
        return {"ctx": 2 * peer[i] + core}

    slots = []
    for chunk in OFFSETS:
        for d in chunk:
            for flip in (0, 1):
                slots.append((d, flip))

    def exp_at(d, flip):
        return 2 * lax.rem(z + d + 16, 16) + (1 - low if flip else low)

    started = []
    counts = {"send": 0, "recv": 0, "local": 0}

    def take(kind, n):
        first = counts[kind]
        counts[kind] += n
        assert counts[kind] <= {"send": SENDS, "recv": RECVS, "local": 8}[kind]
        return first

    def send(src, dst, recv, device):
        copy = pltpu.make_async_remote_copy(
            src_ref=src,
            dst_ref=dst,
            send_sem=send_sems.at[take("send", 1)],
            recv_sem=recv_sems.at[recv],
            device_id=device,
            device_id_type=MESH,
        )
        copy.start()
        started.append(copy)

    def arrive(dst, recv):
        pltpu.make_async_remote_copy(
            src_ref=dst,
            dst_ref=dst,
            send_sem=send_sems.at[0],
            recv_sem=recv_sems.at[recv],
            device_id=partner,
            device_id_type=MESH,
        ).wait_recv()

    class Gather:
        def __init__(self, at):
            self.at = at
            self.base = take("recv", 2 * PLANES)

        def put(self, source, half, i):
            ref = self.at(source, half)
            send(ref, ref, self.base + 2 * source + half, plane(i))

        def wait(self, i, half):
            arrive(self.at(peer[i], half), self.base + 2 * peer[i] + half)

        def start(self, half):
            for i in (1,) + YS if half == 0 else YS + (1,):
                self.put(p, half, i)

        def forward(self):
            self.wait(1, 0)
            for i in YS:
                self.put(peer[1], 0, i)
            for i in YS:
                self.wait(i, 1)
                self.put(peer[i], 1, 1)

        def finish(self):
            for i in YS:
                self.wait(i, 0)
            self.wait(1, 1)
            for i in YS:
                self.wait(i + 1, 0)
                self.wait(i + 1, 1)

    barrier = pltpu.get_barrier_semaphore()
    pl.semaphore_signal(barrier, inc=1, device_id=partner, device_id_type=MESH)
    for i in range(1, PLANES):
        pl.semaphore_signal(barrier, inc=1, device_id=plane(i), device_id_type=MESH)
    for d, flip in slots[1:]:
        pl.semaphore_signal(
            barrier, inc=1, device_id={"exp": exp_at(d, flip)}, device_id_type=MESH
        )

    mine96 = pl.ds(pl.multiple_of(core * UNITS, 16), UNITS)
    head192 = pl.ds(0, 2 * UNITS)
    own_half = pl.ds(pl.multiple_of(core * 2048, 16), 2048)
    other_half = pl.ds(pl.multiple_of(other * 2048, 16), 2048)
    locals_ = []
    for src, dst in (
        (out_proj_hbm.at[own_half], w_out.at[core]),
        (gate_hbm, w_gate.at[mine96]),
        (up_hbm, w_up.at[mine96]),
        (down_hbm, w_down.at[core, :, head192]),
    ):
        copy = pltpu.make_async_copy(src, dst, local_sems.at[take("local", 1)])
        copy.start()
        locals_.append(copy)

    first = core == 0
    length = length_ref[0]
    block_mine = block_ref[ctx]
    block_other = block_ref[2 * p + other]
    position = (iota((TOK, HD), 0) + (length + block_mine * TOK)).astype(F32)
    angles = position * rates_ref[...]
    cosine = jnp.cos(angles)
    sine = jnp.where(iota((TOK, HD), 1) < HD // 2, -1.0, 1.0) * jnp.sin(angles)

    def rope(v):
        v = v.astype(F32)
        return (v * cosine + pltpu.roll(v, HD // 2, 1) * sine).astype(BF)

    for g in range(GROUP):
        low_head = rope(query_ref[:, g * HD : (g + 1) * HD])
        high_head = rope(query_ref[:, (GROUP + g) * HD : (GROUP + g + 1) * HD])
        q_buf[g * TOK : (g + 1) * TOK] = jnp.where(first, low_head, high_head)
        q_stage[g * TOK : (g + 1) * TOK] = jnp.where(first, high_head, low_head)
    for which, cached_ref, new_ref in ((0, cache_key_ref, key_new_ref), (1, cache_value_ref, value_new_ref)):
        old = [cached_ref[:, n * HD : (n + 1) * HD] for n in (0, 1)]
        new = [new_ref[:, n * HD : (n + 1) * HD] for n in (0, 1)]
        if which == 0:
            new = [rope(v) for v in new]
        kv[p, 0, which, :CACHED] = jnp.where(first, old[0], old[1])
        kv[p, 0, which, CACHED:] = jnp.where(first, new[0], new[1])
        kv_stage[which, :CACHED] = jnp.where(first, old[1], old[0])
        kv_stage[which, CACHED:] = jnp.where(first, new[1], new[0])

    logits = logits_ref[...]
    powers = jnp.exp(logits - jnp.max(logits, axis=1, keepdims=True))
    shares = powers / jnp.sum(powers, axis=1, keepdims=True)
    routes = routes_ref[...]
    lane = iota((TOK, 128), 1)
    token = iota((TOK, 128), 0)
    taken = jnp.zeros((TOK, 128), F32)
    share = jnp.zeros((TOK, 128), F32)
    for x in range(8):
        hit = routes[:, x : x + 1] == lane
        taken = jnp.where(hit, 1.0, taken)
        share = share + jnp.where(hit, shares[:, x : x + 1], 0.0)
    rank = taken
    for step in (1, 2, 4, 8):
        rank = rank + jnp.where(token >= step, pltpu.roll(rank, step, 0), 0.0)
    row_of = jnp.where(taken > 0.0, rank - 1.0, -1.0)
    info[p, 0] = row_of
    info[p, 1] = share

    pl.semaphore_wait(barrier, PLANES + len(slots) - 1)

    kv_gather = Gather(lambda source, half: kv.at[source, half])
    pair_kv, pair_q = take("recv", 1), take("recv", 1)
    send(kv_stage, kv.at[p, 1], pair_kv, partner)
    kv_gather.start(0)
    q_theirs = q_buf.at[pl.ds(GROUP * TOK, GROUP * TOK)]
    send(q_stage, q_theirs, pair_q, partner)
    arrive(kv.at[p, 1], pair_kv)
    kv_gather.start(1)
    pair_weights = [take("recv", 1) for _ in range(4)]
    send(out_proj_hbm.at[other_half], w_out.at[core], pair_weights[0], partner)
    send(gate_hbm, w_gate.at[mine96], pair_weights[1], partner)
    send(up_hbm, w_up.at[mine96], pair_weights[2], partner)
    send(down_hbm, w_down.at[core, :, head192], pair_weights[3], partner)
    info_base = take("recv", PLANES)
    for i in range(1, PLANES):
        send(info.at[p], info.at[p], info_base + p, plane(i))

    row8 = jnp.concatenate([row_of.astype(BF)] * PLANES, axis=0)
    s_row, s_lane = iota((512, 128), 0), iota((512, 128), 1)
    spread = dot_t(onehot((s_row >> 4) == s_lane), row8)
    select = onehot(
        (spread == ((s_row >> 3) & 1).astype(F32)) & ((s_row & 7) == (s_lane >> 4))
    )

    scale = HD ** (-0.5)
    arrive(q_theirs, pair_q)
    q_rows = 2 * GROUP * TOK
    QB = 128

    key_lane = iota((1, 256), 1)

    def score(slot, keys, visible_of):
        def step(rb, carry):
            rows = pl.ds(pl.multiple_of(rb * QB, QB), QB)
            s = dot_t(q_buf[rows], keys) * scale
            s = jnp.where(visible_of(rb), s, NEG)
            score_buf[slot, rows] = s
            top = jnp.maximum(s[:, :128], s[:, 128:])
            peak_buf[rows] = jnp.maximum(peak_buf[rows], top)
            return carry

        lax.fori_loop(0, q_rows // QB, step, 0)

    def score_cached(i):
        source = peer[i]
        keys = jnp.concatenate([kv[source, 0, 0, :CACHED], kv[source, 1, 0, :CACHED]], axis=0)
        near = (2 * source + core) * CACHED
        far = (2 * source + other) * CACHED
        slot = jnp.where(key_lane < CACHED, near + key_lane, far + key_lane - CACHED)
        visible = slot < length
        score(source, keys, lambda rb: visible)

    peak_buf[...] = jnp.full((q_rows, 128), NEG, F32)
    score_cached(0)
    kv_gather.forward()
    kv_gather.finish()
    for i in (1,) + YS + (3, 7, 5):
        score_cached(i)
    new_keys = jnp.concatenate(
        [kv[s, o, 0, CACHED:] for s in range(PLANES) for o in (0, 1)], axis=0
    )
    new_values = jnp.concatenate(
        [kv[s, o, 1, CACHED:] for s in range(PLANES) for o in (0, 1)], axis=0
    )
    key_offset = jnp.zeros((1, 256), jnp.int32)
    for s in range(PLANES):
        for o in (0, 1):
            block = block_ref[2 * s + (core if o == 0 else other)]
            key_offset = jnp.where((key_lane >> 4) == 2 * s + o, block * TOK, key_offset)
    key_offset = key_offset + (key_lane & 15)

    def causal(rb):
        block = jnp.where(rb < 2, block_mine, block_other)
        return key_offset <= (iota((QB, 256), 0) & 15) + block * TOK

    score(PLANES, new_keys, causal)

    def weigh(rb, carry):
        rows = pl.ds(pl.multiple_of(rb * QB, QB), QB)
        peak = jnp.max(peak_buf[rows], axis=1, keepdims=True)
        total = jnp.zeros((QB, 128), F32)
        mixed = jnp.zeros((QB, HD), F32)
        for s in range(PLANES + 1):
            weights = jnp.exp(score_buf[s, rows] - peak)
            total = total + weights[:, :128] + weights[:, 128:]
            if s < PLANES:
                values = jnp.concatenate([kv[s, 0, 1, :CACHED], kv[s, 1, 1, :CACHED]], axis=0)
            else:
                values = new_values
            mixed = mixed + dot(weights.astype(BF), values)
        mixed = (mixed / jnp.sum(total, axis=1, keepdims=True)).astype(BF)
        q_buf[rows] = mixed
        return carry

    lax.fori_loop(0, q_rows // QB, weigh, 0)
    for o in (0, 1):
        for g in range(GROUP):
            r = (o * GROUP + g) * TOK
            mix[o, p, :, g * HD : (g + 1) * HD] = q_buf[r : r + TOK]

    mix_gather = Gather(lambda source, half: mix.at[half, source])
    mix_gather.start(0)
    mix_gather.start(1)
    mix_gather.forward()
    locals_[0].wait()
    arrive(w_out.at[other], pair_weights[0])
    mix_gather.finish()

    def project(o):
        left = mix[o].reshape(PLANES * TOK, 2048)
        return [dot(left, w_out[half]) for half in (0, 1)]

    pair_part = take("recv", 1)
    theirs = project(1)
    part_send[0] = theirs[0]
    part_send[1] = theirs[1]
    send(part_send, part_recv, pair_part, partner)
    ours = project(0)
    arrive(part_recv, pair_part)
    for half in (0, 1):
        block = (ours[half] + part_recv[half]).astype(BF).reshape(PLANES, TOK, 256)
        proj_send[:, :, half * 256 : (half + 1) * 256] = block
    attn_base = take("recv", PLANES)
    for i in YS + (1, 3, 7, 5):
        send(proj_send.at[peer[i]], attn.at[p], attn_base + p, plane(i))
    attn[p] = proj_send[p]
    for i in range(1, PLANES):
        arrive(attn.at[peer[i]], attn_base + peer[i])

    square = jnp.zeros((TOK, 1), F32)
    streams = []
    for j in range(PLANES):
        cols = slice(j * WIDE, (j + 1) * WIDE)
        v = (resid_ref[:, cols].astype(F32) + attn[j].astype(F32)).astype(BF)
        stream_buf[j] = v
        v = v.astype(F32)
        streams.append(v)
        square = square + jnp.sum(v * v, axis=1, keepdims=True)
    inverse = lax.rsqrt(square * (1.0 / (PLANES * WIDE)) + 1e-06)
    normed = jnp.concatenate(
        [
            (streams[j] * inverse * gain_ref[:, j * WIDE : (j + 1) * WIDE]).astype(BF)
            for j in range(PLANES)
        ],
        axis=0,
    )
    z_send[...] = dot(select, normed).astype(BF).reshape(NEXP, 16, WIDE)

    z_base = take("recv", len(slots))
    z_recv[0] = z_send[ex]
    for n, (d, flip) in enumerate(slots):
        if n > 0:
            to = exp_at(d, flip)
            send(z_send.at[to], z_recv.at[n], z_base + n, {"exp": to})

    for copy in locals_[1:]:
        copy.wait()
    theirs96 = pl.ds(pl.multiple_of(other * UNITS, 16), UNITS)
    arrive(w_gate.at[theirs96], pair_weights[1])
    arrive(w_up.at[theirs96], pair_weights[2])
    arrive(w_down.at[other, :, head192], pair_weights[3])
    w_gate[192:] = w_gate[128:192]
    w_up[192:] = w_up[128:192]
    for o in (0, 1):
        w_down[o, :, 192:] = w_down[o, :, 128:192]

    r_, c_ = iota((128, 128), 0), iota((128, 128), 1)
    to_blocks = onehot(((r_ >> 4) == (c_ & 7)) & ((r_ & 15) == (c_ >> 3)))
    to_requests = onehot(
        ((r_ >> 4) == ((c_ >> 1) & 7)) & (((r_ >> 1) & 7) == (c_ >> 4)) & ((r_ & 1) == (c_ & 1))
    )
    ret_base = take("recv", len(slots))
    row_gathers = [
        Gather(lambda source, half, q=q: rows_buf.at[q, source, pl.ds(4 * half, 4)])
        for q in range(CHUNKS)
    ]
    hid_gathers = [
        Gather(lambda source, half, q=q: hid.at[q, source, pl.ds(UNITS * half, UNITS)])
        for q in range(CHUNKS)
    ]

    def gather_rows(q):
        for n in range(q * PER, (q + 1) * PER):
            if n > 0:
                arrive(z_recv.at[n], z_base + n)
        block = z_recv[q * PER : (q + 1) * PER].reshape(128, WIDE)
        rows_buf[q, p] = dot(to_blocks, block).astype(BF).reshape(PLANES, 16, WIDE)
        row_gathers[q].start(0)
        row_gathers[q].start(1)

    def activate(q):
        row_gathers[q].finish()
        gate = jnp.zeros((ROWS, 256), F32)
        upward = jnp.zeros((ROWS, 256), F32)
        for j in range(PLANES):
            rows = rows_buf[q, :, j].reshape(ROWS, WIDE)
            cols = slice(j * WIDE, (j + 1) * WIDE)
            gate = gate + dot_t(rows, w_gate[:, cols])
            upward = upward + dot_t(rows, w_up[:, cols])
        hidden = (gate / (1.0 + jnp.exp(-gate)) * upward).astype(BF)
        tail = hidden[:, 128:]
        left = iota((64, 128), 1) < 64
        hid[q, p, :128] = hidden[:, :128]
        hid[q, p, 128:] = jnp.where(left, tail[:64], tail[64:])
        hid_gathers[q].start(0)
        hid_gathers[q].start(1)

    def finish_rows(q):
        hid_gathers[q].finish()
        left = iota((64, 128), 1) < 64
        result = [jnp.zeros((ROWS, 256), F32) for _ in (0, 1)]
        zero = jnp.zeros((64, 128), BF)
        for s in range(PLANES):
            tail = hid[q, s, 128:]
            tail = jnp.concatenate(
                [jnp.where(left, tail, zero), jnp.where(left, zero, tail)], axis=0
            )
            hidden = jnp.concatenate([hid[q, s, :128], tail], axis=1)
            for o in (0, 1):
                result[o] = result[o] + dot(hidden, w_down[o, s])
        for o in (0, 1):
            block = dot(to_requests, result[o].astype(BF)).astype(BF).reshape(PER, 16, 256)
            ret_send[q * PER : (q + 1) * PER, :, o * 256 : (o + 1) * 256] = block
        for n in range(q * PER, (q + 1) * PER):
            d, flip = slots[n]
            if n > 0:
                send(ret_send.at[n], ret.at[ex], ret_base + n, {"exp": exp_at(-d, flip)})
            else:
                ret[ex] = ret_send[0]

    gather_rows(0)
    row_gathers[0].forward()
    gather_rows(1)
    row_gathers[1].forward()
    activate(0)
    gather_rows(2)
    row_gathers[2].forward()
    hid_gathers[0].forward()
    activate(1)
    finish_rows(0)
    gather_rows(3)
    row_gathers[3].forward()
    hid_gathers[1].forward()
    activate(2)
    finish_rows(1)
    hid_gathers[2].forward()
    activate(3)
    finish_rows(2)
    hid_gathers[3].forward()

    for i in range(1, PLANES):
        arrive(info.at[peer[i]], info_base + peer[i])
    e_row, e_col = iota((128, 512), 0), iota((128, 512), 1)
    pick = onehot(e_row == (e_col >> 4))
    chosen = dot(info[:, 0].reshape(128, 128).astype(BF), pick)
    meets = (chosen == (e_col & 1).astype(F32)) & ((e_row >> 4) == ((e_col >> 1) & 7))
    mixing = [
        jnp.where(meets, dot(part, pick), 0.0).astype(BF)
        for part in thirds(info[:, 1].reshape(128, 128))
    ]

    finish_rows(3)
    for n, (d, flip) in enumerate(slots):
        if n > 0:
            arrive(ret.at[exp_at(d, flip)], ret_base + n)
    returned = ret[...].reshape(512, WIDE)
    added = dot(mixing[0], returned) + dot(mixing[1], returned) + dot(mixing[2], returned)
    fin_send[...] = added.astype(BF).reshape(PLANES, TOK, WIDE)
    fin_base = take("recv", PLANES)
    for i in YS + (1, 3, 7, 5):
        send(fin_send.at[peer[i]], fin.at[p], fin_base + p, plane(i))
    fin[p] = fin_send[p]
    for i in range(1, PLANES):
        arrive(fin.at[peer[i]], fin_base + peer[i])
    for j in range(PLANES):
        total = stream_buf[j].astype(F32) + fin[j].astype(F32)
        out_ref[:, j * WIDE : (j + 1) * WIDE] = total.astype(BF)
    for copy in started:
        copy.wait_send()


def local(
    resid,
    query,
    key_new,
    value_new,
    cache_key,
    cache_value,
    cache_len,
    block_of,
    out_proj,
    norm_gain,
    routes,
    route_logits,
    w_gate,
    w_up,
    w_down,
):
    rates = np.exp(np.arange(HD // 2, dtype=np.float64) * (-2.0 * math.log(1000000.0) / HD))
    rates = jnp.asarray(np.concatenate([rates, rates])[None, :].astype(np.float32))
    smem = pl.BlockSpec(memory_space=pltpu.SMEM)
    vmem = pl.BlockSpec(memory_space=pltpu.VMEM)
    hbm = pl.BlockSpec(memory_space=pl.ANY)
    q_rows = 2 * GROUP * TOK
    scratch = [
        pltpu.VMEM((q_rows, HD), BF),
        pltpu.VMEM((GROUP * TOK, HD), BF),
        pltpu.VMEM((PLANES, 2, 2, KEYS, HD), BF),
        pltpu.VMEM((2, KEYS, HD), BF),
        pltpu.VMEM((PLANES + 1, q_rows, 256), F32),
        pltpu.VMEM((q_rows, 128), F32),
        pltpu.VMEM((2, PLANES, TOK, 2048), BF),
        pltpu.VMEM((2, 2048, 256), BF),
        pltpu.VMEM((2, PLANES * TOK, 256), F32),
        pltpu.VMEM((2, PLANES * TOK, 256), F32),
        pltpu.VMEM((PLANES, TOK, WIDE), BF),
        pltpu.VMEM((PLANES, TOK, WIDE), BF),
        pltpu.VMEM((PLANES, TOK, WIDE), BF),
        pltpu.VMEM((PLANES, 2, TOK, 128), F32),
        pltpu.VMEM((NEXP, 16, WIDE), BF),
        pltpu.VMEM((NEXP, 16, WIDE), BF),
        pltpu.VMEM((CHUNKS, PLANES, PLANES, 16, WIDE), BF),
        pltpu.VMEM((256, 4096), BF),
        pltpu.VMEM((256, 4096), BF),
        pltpu.VMEM((2, PLANES, 256, 256), BF),
        pltpu.VMEM((CHUNKS, PLANES, 192, 128), BF),
        pltpu.VMEM((NEXP, 16, WIDE), BF),
        pltpu.VMEM((NEXP, 16, WIDE), BF),
        pltpu.VMEM((PLANES, TOK, WIDE), BF),
        pltpu.VMEM((PLANES, TOK, WIDE), BF),
        pltpu.SemaphoreType.DMA((SENDS,)),
        pltpu.SemaphoreType.DMA((RECVS,)),
        pltpu.SemaphoreType.DMA((8,)),
    ]
    out = pl.pallas_call(
        kernel,
        out_shape=jax.ShapeDtypeStruct((TOK, 4096), BF),
        in_specs=[smem, smem] + [vmem] * 10 + [hbm] * 4,
        out_specs=vmem,
        scratch_shapes=scratch,
        compiler_params=pltpu.CompilerParams(
            collective_id=0, has_side_effects=True, vmem_limit_bytes=56 * 2**20
        ),
        name="layer",
    )(
        cache_len,
        block_of,
        rates,
        resid[0],
        query[0],
        key_new[0],
        value_new[0],
        cache_key[0],
        cache_value[0],
        norm_gain[None, :],
        routes[0],
        route_logits[0],
        out_proj,
        w_gate[0],
        w_up[0],
        w_down[0].reshape(PLANES, 192, 256),
    )
    return out[None]


def solution(mesh):
    rows = P("exp", "ctx", None)
    in_specs = (
        rows,
        rows,
        rows,
        rows,
        rows,
        rows,
        P("exp"),
        P(),
        P(None, "ctx"),
        P(),
        rows,
        rows,
        rows,
        rows,
        P("exp", None, "ctx"),
    )
    return jax.shard_map(local, mesh=mesh, in_specs=in_specs, out_specs=rows, check_vma=False)
```

time: 497 us -> 153 us (0.31)
  the two profiles are of different devices: /device:TPU:2 before, /device:TPU:8 now
where the time goes in v1:
time: 153 us
  Pallas kernels  148 us (97%)
  local copies, waits for them, and re-layouts  4.27 us (3%)
    pallas_call x1, Pallas kernels, local(): pl.pallas_call(kernel, out_shape=jax.ShapeDtypeStruct((TOK, 4096), BF), i...  148 us

profile of v1, /device:TPU:8, one launch (start us, length us, event | category | flops | bytes accessed | tf_op | source)
XLA Modules:
  0.0 152.5 jit_solution(7836111492694935081)
XLA Ops:
  0.7 1.4 copy.17.routes_ref
  2.0 1.4 copy.18.logits_ref
  3.4 147.6 %layer.1 = bf16[16,4096]{1,0:T(8,128)(2,1)} custom-call(s32[1]{0:T(128)S(6)} %copy.20.length_ref, s32[16]{0:T(128)} %block_ref.1, f32[1,128]{1,0:T(1,128)} %constant.2.clone.rates_ref, bf16[16,4096]{1,0:T(8,128)(2,1)} %bitcast.17, bf16[16,4096]{1,0:T(8,128)(2,1)} %bitcast.18, bf16[16,256]{1,0:T(8,128)(2,1)} %bitcast.22, bf16[16,256]{1,0:T(8,128)(2,1)} %bitcast.23, ...), custom_call_target="tpu_custom_call" | custom-call | tf_op jit(solution)/shard_map/layer/pallas_call | solution.py:595
  151.0 1.6 %copy.21 = bf16[1,16,4096]{2,1,0:T(8,128)(2,1)} copy(bf16[1,16,4096]{2,1,0:T(8,128)(2,1)} %bitcast.16) | data formatting | bytes 262144

commit v2 on v1

--- a/solution.py
+++ b/solution.py
@@ -20,14 +20,14 @@
 WIDE = 512
 NEXP = 32
 UNITS = 96
-OFFSETS = ((0, 1, -1, 2), (8, 7, -7, -6), (6, 5, -5, -4), (4, 3, -3, -2))
+OFFSETS = ((0, 1, -1, 2), (6, 5, -5, -4), (8, 7, -7, -6), (4, 3, -3, -2))
 CHUNKS = len(OFFSETS)
 PER = 8
 ROWS = PER * 2 * PLANES
 YS = (2, 6, 4)
 NEG = -1e30
-SENDS = 288
-RECVS = 320
+SENDS = 304
+RECVS = 336
 
 
 def iota(shape, axis):
@@ -54,23 +54,35 @@
 
 
 def kernel(
+    length_hbm,
+    block_hbm,
+    rates_hbm,
+    query_hbm,
+    key_new_hbm,
+    value_new_hbm,
+    cache_key_hbm,
+    cache_value_hbm,
+    resid_hbm,
+    gain_hbm,
+    routes_hbm,
+    logits_hbm,
+    out_proj_hbm,
+    gate_hbm,
+    up_hbm,
+    down_hbm,
+    out_ref,
     length_ref,
     block_ref,
     rates_ref,
-    resid_ref,
     query_ref,
     key_new_ref,
     value_new_ref,
     cache_key_ref,
     cache_value_ref,
+    resid_ref,
     gain_ref,
     routes_ref,
     logits_ref,
-    out_proj_hbm,
-    gate_hbm,
-    up_hbm,
-    down_hbm,
-    out_ref,
     q_buf,
     q_stage,
     kv,
@@ -78,9 +90,8 @@
     score_buf,
     peak_buf,
     mix,
+    mix_stage,
     w_out,
-    part_send,
-    part_recv,
     proj_send,
     attn,
     stream_buf,
@@ -128,7 +139,7 @@
     def take(kind, n):
         first = counts[kind]
         counts[kind] += n
-        assert counts[kind] <= {"send": SENDS, "recv": RECVS, "local": 8}[kind]
+        assert counts[kind] <= {"send": SENDS, "recv": RECVS, "local": 16}[kind]
         return first
 
     def send(src, dst, recv, device):
@@ -165,9 +176,18 @@
         def wait(self, i, half):
             arrive(self.at(peer[i], half), self.base + 2 * peer[i] + half)
 
-        def start(self, half):
-            for i in (1,) + YS if half == 0 else YS + (1,):
+        def start(self):
+            self.put(p, 0, 1)
+
+        def spread(self, half):
+            for i in YS:
                 self.put(p, half, i)
+
+        def rest(self):
+            for half in (1, 0):
+                for i in YS:
+                    self.put(p, half, i)
+            self.put(p, 1, 1)
 
         def forward(self):
             self.wait(1, 0)
@@ -194,13 +214,29 @@
             barrier, inc=1, device_id={"exp": exp_at(d, flip)}, device_id_type=MESH
         )
 
+    loads = []
+    for src, dst in (
+        (length_hbm, length_ref),
+        (block_hbm, block_ref),
+        (cache_key_hbm, cache_key_ref),
+        (cache_value_hbm, cache_value_ref),
+        (rates_hbm, rates_ref),
+        (key_new_hbm, key_new_ref),
+        (value_new_hbm, value_new_ref),
+        (query_hbm, query_ref),
+        (routes_hbm, routes_ref),
+        (logits_hbm, logits_ref),
+        (resid_hbm, resid_ref),
+        (gain_hbm, gain_ref),
+    ):
+        copy = pltpu.make_async_copy(src, dst, local_sems.at[take("local", 1)])
+        copy.start()
+        loads.append(copy)
     mine96 = pl.ds(pl.multiple_of(core * UNITS, 16), UNITS)
     head192 = pl.ds(0, 2 * UNITS)
-    own_half = pl.ds(pl.multiple_of(core * 2048, 16), 2048)
-    other_half = pl.ds(pl.multiple_of(other * 2048, 16), 2048)
     locals_ = []
     for src, dst in (
-        (out_proj_hbm.at[own_half], w_out.at[core]),
+        (out_proj_hbm, w_out.at[core]),
         (gate_hbm, w_gate.at[mine96]),
         (up_hbm, w_up.at[mine96]),
         (down_hbm, w_down.at[core, :, head192]),
@@ -210,18 +246,22 @@
         locals_.append(copy)
 
     first = core == 0
+    for copy in loads[:2]:
+        copy.wait()
     length = length_ref[0]
     block_mine = block_ref[ctx]
     block_other = block_ref[2 * p + other]
     position = (iota((TOK, HD), 0) + (length + block_mine * TOK)).astype(F32)
+
+    def rope(v):
+        v = v.astype(F32)
+        return (v * cosine + pltpu.roll(v, HD // 2, 1) * sine).astype(BF)
+
+    for copy in loads[2:10]:
+        copy.wait()
     angles = position * rates_ref[...]
     cosine = jnp.cos(angles)
     sine = jnp.where(iota((TOK, HD), 1) < HD // 2, -1.0, 1.0) * jnp.sin(angles)
-
-    def rope(v):
-        v = v.astype(F32)
-        return (v * cosine + pltpu.roll(v, HD // 2, 1) * sine).astype(BF)
-
     for g in range(GROUP):
         low_head = rope(query_ref[:, g * HD : (g + 1) * HD])
         high_head = rope(query_ref[:, (GROUP + g) * HD : (GROUP + g + 1) * HD])
@@ -238,21 +278,25 @@
         kv_stage[which, CACHED:] = jnp.where(first, new[1], new[0])
 
     logits = logits_ref[...]
-    powers = jnp.exp(logits - jnp.max(logits, axis=1, keepdims=True))
-    shares = powers / jnp.sum(powers, axis=1, keepdims=True)
-    routes = routes_ref[...]
-    lane = iota((TOK, 128), 1)
-    token = iota((TOK, 128), 0)
-    taken = jnp.zeros((TOK, 128), F32)
-    share = jnp.zeros((TOK, 128), F32)
+    powers = jnp.exp(logits - jnp.max(logits, axis=0, keepdims=True))
+    shares = powers / jnp.sum(powers, axis=0, keepdims=True)
+    routes = jnp.concatenate([routes_ref[...], jnp.full((8, 128 - TOK), -1, jnp.int32)], axis=1)
+    shares = jnp.concatenate([shares, jnp.zeros((8, 128 - TOK), F32)], axis=1)
+    expert = iota((NEXP, 128), 0)
+    token = iota((NEXP, 128), 1)
+    taken = jnp.zeros((NEXP, 128), F32)
+    share = jnp.zeros((NEXP, 128), F32)
     for x in range(8):
-        hit = routes[:, x : x + 1] == lane
+        hit = routes[x : x + 1] == expert
         taken = jnp.where(hit, 1.0, taken)
-        share = share + jnp.where(hit, shares[:, x : x + 1], 0.0)
+        share = share + jnp.where(hit, shares[x : x + 1], 0.0)
     rank = taken
     for step in (1, 2, 4, 8):
-        rank = rank + jnp.where(token >= step, pltpu.roll(rank, step, 0), 0.0)
+        rank = rank + jnp.where(token >= step, pltpu.roll(rank, step, 1), 0.0)
     row_of = jnp.where(taken > 0.0, rank - 1.0, -1.0)
+    rest = jnp.zeros((128 - NEXP, 128), F32)
+    row_of = jnp.concatenate([row_of, rest], axis=0).T[:TOK]
+    share = jnp.concatenate([share, rest], axis=0).T[:TOK]
     info[p, 0] = row_of
     info[p, 1] = share
 
@@ -261,13 +305,13 @@
     kv_gather = Gather(lambda source, half: kv.at[source, half])
     pair_kv, pair_q = take("recv", 1), take("recv", 1)
     send(kv_stage, kv.at[p, 1], pair_kv, partner)
-    kv_gather.start(0)
+    kv_gather.start()
     q_theirs = q_buf.at[pl.ds(GROUP * TOK, GROUP * TOK)]
     send(q_stage, q_theirs, pair_q, partner)
     arrive(kv.at[p, 1], pair_kv)
-    kv_gather.start(1)
+    kv_gather.rest()
     pair_weights = [take("recv", 1) for _ in range(4)]
-    send(out_proj_hbm.at[other_half], w_out.at[core], pair_weights[0], partner)
+    send(out_proj_hbm, w_out.at[core], pair_weights[0], partner)
     send(gate_hbm, w_gate.at[mine96], pair_weights[1], partner)
     send(up_hbm, w_up.at[mine96], pair_weights[2], partner)
     send(down_hbm, w_down.at[core, :, head192], pair_weights[3], partner)
@@ -313,8 +357,14 @@
     peak_buf[...] = jnp.full((q_rows, 128), NEG, F32)
     score_cached(0)
     kv_gather.forward()
-    kv_gather.finish()
-    for i in (1,) + YS + (3, 7, 5):
+    for i in YS:
+        kv_gather.wait(i, 0)
+        score_cached(i)
+    kv_gather.wait(1, 1)
+    score_cached(1)
+    for i in (3, 7, 5):
+        kv_gather.wait(i, 0)
+        kv_gather.wait(i, 1)
         score_cached(i)
     new_keys = jnp.concatenate(
         [kv[s, o, 0, CACHED:] for s in range(PLANES) for o in (0, 1)], axis=0
@@ -352,34 +402,33 @@
         q_buf[rows] = mixed
         return carry
 
-    lax.fori_loop(0, q_rows // QB, weigh, 0)
-    for o in (0, 1):
+    def mix_half(o, ref):
+        lax.fori_loop(2 * o, 2 * o + 2, weigh, 0)
         for g in range(GROUP):
             r = (o * GROUP + g) * TOK
-            mix[o, p, :, g * HD : (g + 1) * HD] = q_buf[r : r + TOK]
-
+            ref[:, g * HD : (g + 1) * HD] = q_buf[r : r + TOK]
+
+    pair_mix = take("recv", 1)
     mix_gather = Gather(lambda source, half: mix.at[half, source])
-    mix_gather.start(0)
-    mix_gather.start(1)
+    mix_half(1, mix_stage)
+    send(mix_stage, mix.at[1, p], pair_mix, partner)
+    mix_half(0, mix.at[0, p])
+    mix_gather.start()
+    arrive(mix.at[1, p], pair_mix)
+    mix_gather.rest()
     mix_gather.forward()
     locals_[0].wait()
     arrive(w_out.at[other], pair_weights[0])
-    mix_gather.finish()
-
-    def project(o):
-        left = mix[o].reshape(PLANES * TOK, 2048)
-        return [dot(left, w_out[half]) for half in (0, 1)]
-
-    pair_part = take("recv", 1)
-    theirs = project(1)
-    part_send[0] = theirs[0]
-    part_send[1] = theirs[1]
-    send(part_send, part_recv, pair_part, partner)
-    ours = project(0)
-    arrive(part_recv, pair_part)
-    for half in (0, 1):
-        block = (ours[half] + part_recv[half]).astype(BF).reshape(PLANES, TOK, 256)
-        proj_send[:, :, half * 256 : (half + 1) * 256] = block
+    for i in YS + (3, 7, 5):
+        mix_gather.wait(i, 0)
+    left = mix[0].reshape(PLANES * TOK, 2048)
+    projected = [dot(left, w_out[o, core]) for o in (0, 1)]
+    for i in (1, 3, 7, 5):
+        mix_gather.wait(i, 1)
+    left = mix[1].reshape(PLANES * TOK, 2048)
+    for o in (0, 1):
+        block = projected[o] + dot(left, w_out[o, other])
+        proj_send[:, :, o * 256 : (o + 1) * 256] = block.astype(BF).reshape(PLANES, TOK, 256)
     attn_base = take("recv", PLANES)
     for i in YS + (1, 3, 7, 5):
         send(proj_send.at[peer[i]], attn.at[p], attn_base + p, plane(i))
@@ -387,6 +436,8 @@
     for i in range(1, PLANES):
         arrive(attn.at[peer[i]], attn_base + peer[i])
 
+    for copy in loads[10:]:
+        copy.wait()
     square = jnp.zeros((TOK, 1), F32)
     streams = []
     for j in range(PLANES):
@@ -445,8 +496,8 @@
                 arrive(z_recv.at[n], z_base + n)
         block = z_recv[q * PER : (q + 1) * PER].reshape(128, WIDE)
         rows_buf[q, p] = dot(to_blocks, block).astype(BF).reshape(PLANES, 16, WIDE)
-        row_gathers[q].start(0)
-        row_gathers[q].start(1)
+        row_gathers[q].start()
+        row_gathers[q].rest()
 
     def activate(q):
         row_gathers[q].finish()
@@ -462,8 +513,10 @@
         left = iota((64, 128), 1) < 64
         hid[q, p, :128] = hidden[:, :128]
         hid[q, p, 128:] = jnp.where(left, tail[:64], tail[64:])
-        hid_gathers[q].start(0)
-        hid_gathers[q].start(1)
+        hid_gathers[q].start()
+        hid_gathers[q].spread(0)
+        hid_gathers[q].spread(1)
+        hid_gathers[q].put(p, 1, 1)
 
     def finish_rows(q):
         hid_gathers[q].finish()
@@ -491,18 +544,18 @@
     gather_rows(0)
     row_gathers[0].forward()
     gather_rows(1)
+    activate(0)
     row_gathers[1].forward()
-    activate(0)
+    hid_gathers[0].forward()
     gather_rows(2)
-    row_gathers[2].forward()
-    hid_gathers[0].forward()
     activate(1)
     finish_rows(0)
+    row_gathers[2].forward()
+    hid_gathers[1].forward()
     gather_rows(3)
-    row_gathers[3].forward()
-    hid_gathers[1].forward()
     activate(2)
     finish_rows(1)
+    row_gathers[3].forward()
     hid_gathers[2].forward()
     activate(3)
     finish_rows(2)
@@ -520,6 +573,9 @@
     ]
 
     finish_rows(3)
+    for copy in started:
+        copy.wait_send()
+    started.clear()
     for n, (d, flip) in enumerate(slots):
         if n > 0:
             arrive(ret.at[exp_at(d, flip)], ret_base + n)
@@ -558,11 +614,22 @@
 ):
     rates = np.exp(np.arange(HD // 2, dtype=np.float64) * (-2.0 * math.log(1000000.0) / HD))
     rates = jnp.asarray(np.concatenate([rates, rates])[None, :].astype(np.float32))
-    smem = pl.BlockSpec(memory_space=pltpu.SMEM)
     vmem = pl.BlockSpec(memory_space=pltpu.VMEM)
     hbm = pl.BlockSpec(memory_space=pl.ANY)
     q_rows = 2 * GROUP * TOK
     scratch = [
+        pltpu.SMEM((1,), jnp.int32),
+        pltpu.SMEM((16,), jnp.int32),
+        pltpu.VMEM((1, HD), F32),
+        pltpu.VMEM((TOK, 4096), BF),
+        pltpu.VMEM((TOK, 256), BF),
+        pltpu.VMEM((TOK, 256), BF),
+        pltpu.VMEM((CACHED, 256), BF),
+        pltpu.VMEM((CACHED, 256), BF),
+        pltpu.VMEM((TOK, 4096), BF),
+        pltpu.VMEM((1, 4096), F32),
+        pltpu.VMEM((8, TOK), jnp.int32),
+        pltpu.VMEM((8, TOK), F32),
         pltpu.VMEM((q_rows, HD), BF),
         pltpu.VMEM((GROUP * TOK, HD), BF),
         pltpu.VMEM((PLANES, 2, 2, KEYS, HD), BF),
@@ -570,9 +637,8 @@
         pltpu.VMEM((PLANES + 1, q_rows, 256), F32),
         pltpu.VMEM((q_rows, 128), F32),
         pltpu.VMEM((2, PLANES, TOK, 2048), BF),
-        pltpu.VMEM((2, 2048, 256), BF),
-        pltpu.VMEM((2, PLANES * TOK, 256), F32),
-        pltpu.VMEM((2, PLANES * TOK, 256), F32),
+        pltpu.VMEM((TOK, 2048), BF),
+        pltpu.VMEM((2, 2, 2048, 256), BF),
         pltpu.VMEM((PLANES, TOK, WIDE), BF),
         pltpu.VMEM((PLANES, TOK, WIDE), BF),
         pltpu.VMEM((PLANES, TOK, WIDE), BF),
@@ -590,12 +656,12 @@
         pltpu.VMEM((PLANES, TOK, WIDE), BF),
         pltpu.SemaphoreType.DMA((SENDS,)),
         pltpu.SemaphoreType.DMA((RECVS,)),
-        pltpu.SemaphoreType.DMA((8,)),
+        pltpu.SemaphoreType.DMA((16,)),
     ]
     out = pl.pallas_call(
         kernel,
         out_shape=jax.ShapeDtypeStruct((TOK, 4096), BF),
-        in_specs=[smem, smem] + [vmem] * 10 + [hbm] * 4,
+        in_specs=[hbm] * 16,
         out_specs=vmem,
         scratch_shapes=scratch,
         compiler_params=pltpu.CompilerParams(
@@ -606,16 +672,16 @@
         cache_len,
         block_of,
         rates,
-        resid[0],
         query[0],
         key_new[0],
         value_new[0],
         cache_key[0],
         cache_value[0],
+        resid[0],
         norm_gain[None, :],
-        routes[0],
-        route_logits[0],
-        out_proj,
+        routes[0].T,
+        route_logits[0].T,
+        out_proj.reshape(2, 2048, 256),
         w_gate[0],
         w_up[0],
         w_down[0].reshape(PLANES, 192, 256),

time: 153 us -> 139 us (0.908)
  the two profiles are of different devices: /device:TPU:8 before, /device:TPU:32 now
where the time goes in v2:
time: 139 us
  Pallas kernels  136 us (98%)
  local copies, waits for them, and re-layouts  1.57 us (1%)
    pallas_call x1, Pallas kernels, local(): pl.pallas_call(kernel, out_shape=jax.ShapeDtypeStruct((TOK, 4096), BF), i...  136 us

profile of v2, /device:TPU:32, one launch (start us, length us, event | category | flops | bytes accessed | tf_op | source)
XLA Modules:
  0.0 138.7 jit_solution(10293941804729195947)
XLA Ops:
  0.7 136.5 %layer.1 = bf16[16,4096]{1,0:T(8,128)(2,1)} custom-call(s32[1]{0:T(128)S(6)} %copy.18.length_hbm, s32[16]{0:T(128)} %block_hbm.1, f32[1,128]{1,0:T(1,128)} %constant.2.clone.rates_hbm, bf16[16,4096]{1,0:T(8,128)(2,1)} %bitcast.23, bf16[16,256]{1,0:T(8,128)(2,1)} %bitcast.28, bf16[16,256]{1,0:T(8,128)(2,1)} %bitcast.29, bf16[128,256]{1,0:T(8,128)(2,1)} %bitcast.25, ...), custom_call_target="tpu_custom_call" | custom-call | tf_op jit(solution)/shard_map/layer/pallas_call | solution.py:661
  137.1 1.6 %copy.19 = bf16[1,16,4096]{2,1,0:T(8,128)(2,1)} copy(bf16[1,16,4096]{2,1,0:T(8,128)(2,1)} %bitcast.22) | data formatting | bytes 262144

commit v3 on v2

--- a/solution.py
+++ b/solution.py
@@ -20,7 +20,7 @@
 WIDE = 512
 NEXP = 32
 UNITS = 96
-OFFSETS = ((0, 1, -1, 2), (6, 5, -5, -4), (8, 7, -7, -6), (4, 3, -3, -2))
+OFFSETS = ((0, 1, -1, -2), (6, 5, -5, -4), (8, 7, -7, -6), (4, 3, -3, 2))
 CHUNKS = len(OFFSETS)
 PER = 8
 ROWS = PER * 2 * PLANES
@@ -98,7 +98,11 @@
     info,
     z_send,
     z_recv,
+    rows_send,
     rows_buf,
+    sum_send,
+    sum_recv,
+    sum_own,
     w_gate,
     w_up,
     w_down,
@@ -178,10 +182,13 @@
 
         def start(self):
             self.put(p, 0, 1)
-
-        def spread(self, half):
-            for i in YS:
-                self.put(p, half, i)
+            for half in (0, 1):
+                for i in YS:
+                    self.put(p, half, i)
+            self.put(p, 1, 1)
+
+        def first(self):
+            self.put(p, 0, 1)
 
         def rest(self):
             for half in (1, 0):
@@ -204,6 +211,48 @@
             for i in YS:
                 self.wait(i + 1, 0)
                 self.wait(i + 1, 1)
+
+    class RowGather:
+        def __init__(self, q):
+            self.q = q
+            self.base = take("recv", PLANES)
+
+        def put(self, i, to):
+            ref = rows_buf.at[self.q, peer[i]]
+            send(ref, ref, self.base + peer[i], plane(to))
+
+        def wait(self, i):
+            arrive(rows_buf.at[self.q, peer[i]], self.base + peer[i])
+
+        def start(self):
+            send(rows_send.at[self.q], rows_buf.at[self.q, p], self.base + p, plane(1))
+            for i in YS:
+                self.put(0, i)
+
+        def forward(self):
+            self.wait(1)
+            for i in YS:
+                self.put(1, i)
+
+        def finish(self):
+            for i in YS + (3, 7, 5):
+                self.wait(i)
+
+    class Direct:
+        def __init__(self, at):
+            self.at = at
+            self.base = take("recv", PLANES)
+
+        def start(self):
+            for i in YS + (1, 3, 7, 5):
+                send(self.at(p), self.at(p), self.base + p, plane(i))
+
+        def forward(self):
+            pass
+
+        def finish(self):
+            for i in YS + (1, 3, 7, 5):
+                arrive(self.at(peer[i]), self.base + peer[i])
 
     barrier = pltpu.get_barrier_semaphore()
     pl.semaphore_signal(barrier, inc=1, device_id=partner, device_id_type=MESH)
@@ -234,11 +283,13 @@
         loads.append(copy)
     mine96 = pl.ds(pl.multiple_of(core * UNITS, 16), UNITS)
     head192 = pl.ds(0, 2 * UNITS)
+    near_cols = pl.ds(pl.multiple_of(h * 2048, 2048), 2048)
+    far_cols = pl.ds(pl.multiple_of((1 - h) * 2048, 2048), 2048)
     locals_ = []
     for src, dst in (
         (out_proj_hbm, w_out.at[core]),
-        (gate_hbm, w_gate.at[mine96]),
-        (up_hbm, w_up.at[mine96]),
+        (gate_hbm.at[:, near_cols], w_gate.at[0, mine96]),
+        (up_hbm.at[:, near_cols], w_up.at[0, mine96]),
         (down_hbm, w_down.at[core, :, head192]),
     ):
         copy = pltpu.make_async_copy(src, dst, local_sems.at[take("local", 1)])
@@ -305,16 +356,28 @@
     kv_gather = Gather(lambda source, half: kv.at[source, half])
     pair_kv, pair_q = take("recv", 1), take("recv", 1)
     send(kv_stage, kv.at[p, 1], pair_kv, partner)
-    kv_gather.start()
+    kv_gather.first()
     q_theirs = q_buf.at[pl.ds(GROUP * TOK, GROUP * TOK)]
     send(q_stage, q_theirs, pair_q, partner)
     arrive(kv.at[p, 1], pair_kv)
     kv_gather.rest()
     pair_weights = [take("recv", 1) for _ in range(4)]
     send(out_proj_hbm, w_out.at[core], pair_weights[0], partner)
-    send(gate_hbm, w_gate.at[mine96], pair_weights[1], partner)
-    send(up_hbm, w_up.at[mine96], pair_weights[2], partner)
+    send(gate_hbm.at[:, near_cols], w_gate.at[0, mine96], pair_weights[1], partner)
+    send(up_hbm.at[:, near_cols], w_up.at[0, mine96], pair_weights[2], partner)
     send(down_hbm, w_down.at[core, :, head192], pair_weights[3], partner)
+    cross_weights = [take("recv", 1) for _ in range(8)]
+
+    def cross(piece):
+        src, dst = ((gate_hbm, w_gate), (up_hbm, w_up))[piece // 2]
+        rows = pl.ds(48 * (piece % 2), 48)
+        to = pl.ds(pl.multiple_of(core * UNITS + 48 * (piece % 2), 16), 48)
+        send(src.at[rows, far_cols], dst.at[1, to], cross_weights[piece], plane(1))
+
+    def crossed(piece, whose):
+        dst = (w_gate, w_up)[piece // 2]
+        return dst.at[1, pl.ds(pl.multiple_of(whose * UNITS + 48 * (piece % 2), 16), 48)]
+
     info_base = take("recv", PLANES)
     for i in range(1, PLANES):
         send(info.at[p], info.at[p], info_base + p, plane(i))
@@ -357,6 +420,8 @@
     peak_buf[...] = jnp.full((q_rows, 128), NEG, F32)
     score_cached(0)
     kv_gather.forward()
+    cross(0)
+    cross(1)
     for i in YS:
         kv_gather.wait(i, 0)
         score_cached(i)
@@ -413,7 +478,7 @@
     mix_half(1, mix_stage)
     send(mix_stage, mix.at[1, p], pair_mix, partner)
     mix_half(0, mix.at[0, p])
-    mix_gather.start()
+    mix_gather.first()
     arrive(mix.at[1, p], pair_mix)
     mix_gather.rest()
     mix_gather.forward()
@@ -432,6 +497,7 @@
     attn_base = take("recv", PLANES)
     for i in YS + (1, 3, 7, 5):
         send(proj_send.at[peer[i]], attn.at[p], attn_base + p, plane(i))
+    cross(2)
     attn[p] = proj_send[p]
     for i in range(1, PLANES):
         arrive(attn.at[peer[i]], attn_base + peer[i])
@@ -463,60 +529,83 @@
         if n > 0:
             to = exp_at(d, flip)
             send(z_send.at[to], z_recv.at[n], z_base + n, {"exp": to})
-
-    for copy in locals_[1:]:
-        copy.wait()
+        if n == PER - 1:
+            cross(3)
+
     theirs96 = pl.ds(pl.multiple_of(other * UNITS, 16), UNITS)
-    arrive(w_gate.at[theirs96], pair_weights[1])
-    arrive(w_up.at[theirs96], pair_weights[2])
-    arrive(w_down.at[other, :, head192], pair_weights[3])
-    w_gate[192:] = w_gate[128:192]
-    w_up[192:] = w_up[128:192]
-    for o in (0, 1):
-        w_down[o, :, 192:] = w_down[o, :, 128:192]
+
+    def pass_weights(pieces):
+        for piece in pieces:
+            ref = crossed(piece, core)
+            arrive(ref, cross_weights[piece])
+            send(ref, ref, cross_weights[4 + piece], partner)
+
+    def complete_weights():
+        for copy in locals_[1:]:
+            copy.wait()
+        arrive(w_gate.at[0, theirs96], pair_weights[1])
+        arrive(w_up.at[0, theirs96], pair_weights[2])
+        arrive(w_down.at[other, :, head192], pair_weights[3])
+        for piece in range(4):
+            arrive(crossed(piece, other), cross_weights[4 + piece])
+        for side in (0, 1):
+            w_gate[side, 192:] = w_gate[side, 128:192]
+            w_up[side, 192:] = w_up[side, 128:192]
+        for o in (0, 1):
+            w_down[o, :, 192:] = w_down[o, :, 128:192]
 
     r_, c_ = iota((128, 128), 0), iota((128, 128), 1)
-    to_blocks = onehot(((r_ >> 4) == (c_ & 7)) & ((r_ & 15) == (c_ >> 3)))
+    to_blocks = onehot(((((r_ >> 4) + 4 * h) & 7) == (c_ & 7)) & ((r_ & 15) == (c_ >> 3)))
     to_requests = onehot(
         ((r_ >> 4) == ((c_ >> 1) & 7)) & (((r_ >> 1) & 7) == (c_ >> 4)) & ((r_ & 1) == (c_ & 1))
     )
     ret_base = take("recv", len(slots))
-    row_gathers = [
-        Gather(lambda source, half, q=q: rows_buf.at[q, source, pl.ds(4 * half, 4)])
-        for q in range(CHUNKS)
-    ]
+    row_gathers = [RowGather(q) for q in range(CHUNKS)]
+    cross_sums = [take("recv", 1) for _ in range(CHUNKS)]
     hid_gathers = [
         Gather(lambda source, half, q=q: hid.at[q, source, pl.ds(UNITS * half, UNITS)])
-        for q in range(CHUNKS)
+        for q in range(CHUNKS - 1)
     ]
+    hid_gathers.append(Direct(lambda source: hid.at[CHUNKS - 1, source]))
 
     def gather_rows(q):
         for n in range(q * PER, (q + 1) * PER):
             if n > 0:
                 arrive(z_recv.at[n], z_base + n)
         block = z_recv[q * PER : (q + 1) * PER].reshape(128, WIDE)
-        rows_buf[q, p] = dot(to_blocks, block).astype(BF).reshape(PLANES, 16, WIDE)
+        block = dot(to_blocks, block).astype(BF).reshape(PLANES, 16, WIDE)
+        rows_buf[q, p] = block[:4]
+        rows_send[q] = block[4:]
         row_gathers[q].start()
-        row_gathers[q].rest()
+
+    def pack(v):
+        left = iota((64, 128), 1) < 64
+        return jnp.concatenate([v[:, :128], jnp.where(left, v[:64, 128:], v[64:, 128:])], axis=0)
+
+    def multiply(q):
+        row_gathers[q].finish()
+        for side in (1, 0):
+            gate = jnp.zeros((ROWS, 256), F32)
+            upward = jnp.zeros((ROWS, 256), F32)
+            for j in range(4):
+                rows = rows_buf[q, :, j].reshape(ROWS, WIDE)
+                cols = slice(j * WIDE, (j + 1) * WIDE)
+                gate = gate + dot_t(rows, w_gate[side, :, cols])
+                upward = upward + dot_t(rows, w_up[side, :, cols])
+            if side == 1:
+                sum_send[q, 0] = pack(gate).astype(BF)
+                sum_send[q, 1] = pack(upward).astype(BF)
+                send(sum_send.at[q], sum_recv.at[q], cross_sums[q], plane(1))
+            else:
+                sum_own[q, 0] = pack(gate)
+                sum_own[q, 1] = pack(upward)
 
     def activate(q):
-        row_gathers[q].finish()
-        gate = jnp.zeros((ROWS, 256), F32)
-        upward = jnp.zeros((ROWS, 256), F32)
-        for j in range(PLANES):
-            rows = rows_buf[q, :, j].reshape(ROWS, WIDE)
-            cols = slice(j * WIDE, (j + 1) * WIDE)
-            gate = gate + dot_t(rows, w_gate[:, cols])
-            upward = upward + dot_t(rows, w_up[:, cols])
-        hidden = (gate / (1.0 + jnp.exp(-gate)) * upward).astype(BF)
-        tail = hidden[:, 128:]
-        left = iota((64, 128), 1) < 64
-        hid[q, p, :128] = hidden[:, :128]
-        hid[q, p, 128:] = jnp.where(left, tail[:64], tail[64:])
+        arrive(sum_recv.at[q], cross_sums[q])
+        gate = sum_own[q, 0] + sum_recv[q, 0].astype(F32)
+        upward = sum_own[q, 1] + sum_recv[q, 1].astype(F32)
+        hid[q, p] = (gate / (1.0 + jnp.exp(-gate)) * upward).astype(BF)
         hid_gathers[q].start()
-        hid_gathers[q].spread(0)
-        hid_gathers[q].spread(1)
-        hid_gathers[q].put(p, 1, 1)
 
     def finish_rows(q):
         hid_gathers[q].finish()
@@ -542,20 +631,27 @@
                 ret[ex] = ret_send[0]
 
     gather_rows(0)
+    pass_weights((0, 0 + 1))
     row_gathers[0].forward()
+    pass_weights((2, 2 + 1))
     gather_rows(1)
+    complete_weights()
+    multiply(0)
+    row_gathers[1].forward()
+    gather_rows(2)
     activate(0)
-    row_gathers[1].forward()
+    multiply(1)
+    row_gathers[2].forward()
     hid_gathers[0].forward()
-    gather_rows(2)
+    gather_rows(3)
     activate(1)
+    multiply(2)
     finish_rows(0)
-    row_gathers[2].forward()
+    row_gathers[3].forward()
     hid_gathers[1].forward()
-    gather_rows(3)
     activate(2)
+    multiply(3)
     finish_rows(1)
-    row_gathers[3].forward()
     hid_gathers[2].forward()
     activate(3)
     finish_rows(2)
@@ -645,9 +741,13 @@
         pltpu.VMEM((PLANES, 2, TOK, 128), F32),
         pltpu.VMEM((NEXP, 16, WIDE), BF),
         pltpu.VMEM((NEXP, 16, WIDE), BF),
-        pltpu.VMEM((CHUNKS, PLANES, PLANES, 16, WIDE), BF),
-        pltpu.VMEM((256, 4096), BF),
-        pltpu.VMEM((256, 4096), BF),
+        pltpu.VMEM((CHUNKS, 4, 16, WIDE), BF),
+        pltpu.VMEM((CHUNKS, PLANES, 4, 16, WIDE), BF),
+        pltpu.VMEM((CHUNKS, 2, 192, 128), BF),
+        pltpu.VMEM((CHUNKS, 2, 192, 128), BF),
+        pltpu.VMEM((CHUNKS, 2, 192, 128), F32),
+        pltpu.VMEM((2, 256, 2048), BF),
+        pltpu.VMEM((2, 256, 2048), BF),
         pltpu.VMEM((2, PLANES, 256, 256), BF),
         pltpu.VMEM((CHUNKS, PLANES, 192, 128), BF),
         pltpu.VMEM((NEXP, 16, WIDE), BF),

time: 139 us -> 133 us (0.957)
  the two profiles are of different devices: /device:TPU:32 before, /device:TPU:8 now
where the time goes in v3:
time: 133 us
  Pallas kernels  131 us (98%)
  local copies, waits for them, and re-layouts  1.57 us (1%)
    pallas_call x1, Pallas kernels, local(): pl.pallas_call(kernel, out_shape=jax.ShapeDtypeStruct((TOK, 4096), BF), i...  131 us

profile of v3, /device:TPU:8, one launch (start us, length us, event | category | flops | bytes accessed | tf_op | source)
XLA Modules:
  0.0 133.4 jit_solution(14787099038060839685)
XLA Ops:
  0.7 131.1 %layer.1 = bf16[16,4096]{1,0:T(8,128)(2,1)} custom-call(s32[1]{0:T(128)S(6)} %copy.18.length_hbm, s32[16]{0:T(128)} %block_hbm.1, f32[1,128]{1,0:T(1,128)} %constant.2.clone.rates_hbm, bf16[16,4096]{1,0:T(8,128)(2,1)} %bitcast.23, bf16[16,256]{1,0:T(8,128)(2,1)} %bitcast.28, bf16[16,256]{1,0:T(8,128)(2,1)} %bitcast.29, bf16[128,256]{1,0:T(8,128)(2,1)} %bitcast.25, ...), custom_call_target="tpu_custom_call" | custom-call | tf_op jit(solution)/shard_map/layer/pallas_call | solution.py:761
  131.8 1.6 %copy.19 = bf16[1,16,4096]{2,1,0:T(8,128)(2,1)} copy(bf16[1,16,4096]{2,1,0:T(8,128)(2,1)} %bitcast.22) | data formatting | bytes 262144

commit v4 on v3

--- a/solution.py
+++ b/solution.py
@@ -582,9 +582,10 @@
         left = iota((64, 128), 1) < 64
         return jnp.concatenate([v[:, :128], jnp.where(left, v[:64, 128:], v[64:, 128:])], axis=0)
 
-    def multiply(q):
-        row_gathers[q].finish()
-        for side in (1, 0):
+    def multiply(q, side):
+        if side == 1:
+            row_gathers[q].finish()
+        for side in (side,):
             gate = jnp.zeros((ROWS, 256), F32)
             upward = jnp.zeros((ROWS, 256), F32)
             for j in range(4):
@@ -636,21 +637,25 @@
     pass_weights((2, 2 + 1))
     gather_rows(1)
     complete_weights()
-    multiply(0)
+    multiply(0, 1)
     row_gathers[1].forward()
+    multiply(0, 0)
     gather_rows(2)
     activate(0)
-    multiply(1)
+    multiply(1, 1)
     row_gathers[2].forward()
+    multiply(1, 0)
     hid_gathers[0].forward()
     gather_rows(3)
     activate(1)
-    multiply(2)
+    multiply(2, 1)
+    row_gathers[3].forward()
+    multiply(2, 0)
     finish_rows(0)
-    row_gathers[3].forward()
     hid_gathers[1].forward()
     activate(2)
-    multiply(3)
+    multiply(3, 1)
+    multiply(3, 0)
     finish_rows(1)
     hid_gathers[2].forward()
     activate(3)

time: 133 us -> 133 us (level)
  no operation moved by 1% of the time
where the time goes in v4:
time: 133 us
  Pallas kernels  131 us (98%)
  local copies, waits for them, and re-layouts  1.57 us (1%)
    pallas_call x1, Pallas kernels, local(): pl.pallas_call(kernel, out_shape=jax.ShapeDtypeStruct((TOK, 4096), BF), i...  131 us

profile of v4, /device:TPU:8, one launch (start us, length us, event | category | flops | bytes accessed | tf_op | source)
XLA Modules:
  0.0 133.3 jit_solution(14224584039290747897)
XLA Ops:
  0.7 131.0 %layer.1 = bf16[16,4096]{1,0:T(8,128)(2,1)} custom-call(s32[1]{0:T(128)S(6)} %copy.18.length_hbm, s32[16]{0:T(128)} %block_hbm.1, f32[1,128]{1,0:T(1,128)} %constant.2.clone.rates_hbm, bf16[16,4096]{1,0:T(8,128)(2,1)} %bitcast.23, bf16[16,256]{1,0:T(8,128)(2,1)} %bitcast.28, bf16[16,256]{1,0:T(8,128)(2,1)} %bitcast.29, bf16[128,256]{1,0:T(8,128)(2,1)} %bitcast.25, ...), custom_call_target="tpu_custom_call" | custom-call | tf_op jit(solution)/shard_map/layer/pallas_call | solution.py:766
  131.7 1.6 %copy.19 = bf16[1,16,4096]{2,1,0:T(8,128)(2,1)} copy(bf16[1,16,4096]{2,1,0:T(8,128)(2,1)} %bitcast.22) | data formatting | bytes 262144
